TPU v7x, 32 devices: a whole 2x2x4 slice. The times are simulated.
32 devices in a mesh: gx: 4 (over z), gy: 4 (over x, core), gz: 2 (over y).
Axes of the slice: x: 2, y: 2, z: 4, core: 2. Of those that a mesh axis runs over, the one named last changes fastest.
Arguments:
- blocks: bfloat16 [8192, 64, 448], P(('gx', 'gy', 'gz')), may hold values from -1.1953125 to 1.1953125
- prolong: bfloat16 [8192, 4096], P(('gx', 'gy', 'gz')), may hold values from -0.75 to 0.75
- new_owner: int32 [8192], P(('gx', 'gy', 'gz')), may hold values from 0 to 31, as said below
- arrival: int32 [8192], P(('gx', 'gy', 'gz')), may hold values from 0 to 267, as said below
- columns: int32 [8192, 7], P(('gx', 'gy', 'gz')), may hold values from -1 to 639, as said below
- targets: int32 [8192, 7], P(('gx', 'gy', 'gz')), may hold values from 0 to 223, as said below
- ghost_lists: int32 [32, 6, 64], P(('gx', 'gy', 'gz')), may hold values from 0 to 255
- touched: int32 [32, 224], P(('gx', 'gy', 'gz')), may hold values from 0 to 63
Outputs:
- coarse: float32 [2048, 4096], P(('gx', 'gy', 'gz'))
Inputs may be any that keep to these rules, and one draw needn't show every extreme that they name: `new_owner`: every row's new owner is in the same gz column (same gx and gy index); two devices adjacent along gz swap the same number of rows both ways, between 4 and 6, and some adjacent pair swaps exactly 6; every other pair of distinct devices of a column swaps exactly 2 rows each way; so every device holds 256 rows after the move. `arrival`: below 256: an old row of the same device that stays; else 256 + p * 6 + r, the row of rank r among those that the device of gz index p of the column hands over; every staying and every handed-over row is named once. `columns`: entry 0 is the row's own new local index; entry k >= 1 is -1, a local row below 256, or 256 + (k - 1) * 64 + q, the q-th block sent by the neighbour in direction k - 1, which then exists. `targets`: a value v * 32 + q names, for v = 0, a coarse block of the device itself, and for v >= 1 one owned by its neighbour in direction v - 1, which then exists.
All inputs are finite; a program needn't handle non-finite values.
Results may differ from a plain program's by a relative error of at most 0.0029.
Values may be sent and summed in bfloat16 or wider, within the bound.
A program may use at most 256 MiB of HBM per device.

v0:
```python
import jax
import jax.numpy as jnp
from jax import lax
from jax.sharding import PartitionSpec as P

B = 64
NBR = 7
CAP = 6
GCAP = 64
UCAP = 32
U_DEV = 224
CE_DEV = 64


def shifted(value, axis, by):
    devices = lax.axis_size(axis)
    pairs = [(i, i + by) for i in range(devices) if 0 <= i + by < devices]
    return lax.ppermute(value, axis, pairs)


def rank_within(labels, label_count):
    onehot = (labels[:, None] == jnp.arange(label_count, dtype=jnp.int32)[None, :]).astype(
        jnp.int32
    )
    before = jnp.cumsum(onehot, axis=0) - onehot
    return jnp.sum(before * onehot, axis=1)


def shards(blocks, prolong, new_owner, arrival, columns, targets, ghost_lists, touched):
    row_count = blocks.shape[0]
    row_shape = blocks.shape[1:]
    block_area = prolong.shape[1]
    block_side = B
    layers = lax.axis_size("gz")
    own_layer = lax.axis_index("gz")
    peer_layer = new_owner % layers
    staying = peer_layer == own_layer
    row_ranks = rank_within(peer_layer, layers)
    slot_key = jnp.where(staying, layers * CAP, peer_layer * CAP + row_ranks)
    outgoing = jnp.zeros((layers * CAP + 1,) + row_shape, jnp.bfloat16).at[slot_key].set(blocks)
    incoming = lax.all_to_all(
        outgoing[: layers * CAP], "gz", split_axis=0, concat_axis=0, tiled=True
    )
    row_table = jnp.concatenate([blocks, incoming], axis=0)
    arrived_rows = row_table[arrival]
    strides = (lax.axis_size("gy") * layers, layers, 1)
    outbound = prolong[ghost_lists[0].reshape(-1)].reshape(6, GCAP, block_area)
    ghost_parts = [prolong]
    for facing in range(6):
        stride = strides[facing // 2]
        orient = 1 - 2 * (facing % 2)
        ghost_parts.append(shifted(outbound[facing ^ 1], ("gx", "gy", "gz"), -orient * stride))
    block_table = jnp.concatenate(ghost_parts, axis=0)
    live_mask = columns >= 0
    own_block = prolong.reshape(row_count, block_side, block_side)
    left = jnp.einsum(
        "rba,rbx->rax", own_block, arrived_rows, preferred_element_type=jnp.float32
    ).astype(jnp.bfloat16)
    left = left.reshape(row_count, block_side, NBR, block_side)
    neighbour = block_table[jnp.maximum(columns, 0)].reshape(row_count, NBR, block_side, block_side)
    partial_blocks = jnp.einsum(
        "rakb,rkbc->rkac", left, neighbour, preferred_element_type=jnp.float32
    )
    onehot = (
        (targets[:, :, None] == jnp.arange(U_DEV, dtype=jnp.int32)[None, None, :])
        & live_mask[:, :, None]
    ).astype(jnp.float32)
    slot_sums = jnp.einsum(
        "rku,rkx->ux",
        onehot,
        partial_blocks.reshape(row_count, NBR, block_area),
        precision=lax.Precision.HIGHEST,
        preferred_element_type=jnp.float32,
    )
    touched_here = touched[0]
    collected_blocks = [slot_sums[:UCAP]]
    collected_index = [touched_here[:UCAP]]
    for facing in range(6):
        stride = strides[facing // 2]
        orient = 1 - 2 * (facing % 2)
        first_slot = (facing + 1) * UCAP
        got_blocks, got_index = shifted(
            (
                slot_sums[first_slot : first_slot + UCAP],
                touched_here[first_slot : first_slot + UCAP],
            ),
            ("gx", "gy", "gz"),
            orient * stride,
        )
        collected_blocks.append(got_blocks)
        collected_index.append(got_index)
    gathered_blocks = jnp.concatenate(collected_blocks, axis=0)
    gathered_index = jnp.concatenate(collected_index, axis=0)
    selector = (jnp.arange(CE_DEV, dtype=jnp.int32)[:, None] == gathered_index[None, :]).astype(
        jnp.float32
    )
    return jnp.dot(
        selector,
        gathered_blocks,
        precision=lax.Precision.HIGHEST,
        preferred_element_type=jnp.float32,
    )


def solution(mesh):
    in_specs = (
        P(("gx", "gy", "gz"), None, None),
        P(("gx", "gy", "gz"), None),
        P(("gx", "gy", "gz")),
        P(("gx", "gy", "gz")),
        P(("gx", "gy", "gz"), None),
        P(("gx", "gy", "gz"), None),
        P(("gx", "gy", "gz"), None, None),
        P(("gx", "gy", "gz"), None),
    )
    out_specs = P(("gx", "gy", "gz"), None)
    return jax.shard_map(shards, mesh=mesh, in_specs=in_specs, out_specs=out_specs, check_vma=False)
```

profile of v0, /device:TPU:2, one launch (start us, length us, event | category | flops | bytes accessed | tf_op | source)
XLA Modules:
  0.0 461.9 jit_solution(9491811459108751822)
XLA Ops:
  0.0 0.7 reduce.1
  0.8 9.4 %gather_fusion.1 = bf16[384,4096]{1,0:T(8,128)(2,1)S(1)} fusion(bf16[256,4096]{1,0:T(8,128)(2,1)} %param.9, s32[1024]{0:T(1024)S(1)} %pad_clamp_fusion.1), kind=kCustom, calls=%fused_computation.1 | custom fusion | bytes 6292992 | tf_op jit(solution)/shard_map/gather | solution.py:47
  10.2 1.7 fusion.12
  11.9 1.3 collective-permute-start.6
  13.2 5.4 %collective-permute-start.7 = (bf16[64,4096]{1,0:T(8,128)(2,1)}, bf16[64,4096]{1,0:T(8,128)(2,1)}, u32[]{:S(2)}, u32[]{:S(2)}) collective-permute-start(bf16[64,4096]{1,0:T(8,128)(2,1)} %get-tuple-element.16), channel_id=1, source_target_pairs={{0,8},{1,9},{2,10},{3,11},{4,12},{5,13},{6,14},{7,15},{8,16},{9,17... | collective-permute-start | bytes 1572872 | tf_op jit(solution)/shard_map/ppermute | solution.py:18
  18.5 1.9 collective-permute-start.8
  20.5 2.4 collective-permute-start.9
  22.9 4.1 collective-permute-start.10
  27.0 0.6 reduce-window.6
  27.7 0.2 slice_reduce_fusion
  27.9 0.2 reduce-window.9
  28.1 23.3 %copy.14 = bf16[256,64,448]{2,1,0:T(8,128)(2,1)} copy(bf16[256,64,448]{0,2,1:T(8,128)(2,1)} %param.8) | data formatting | bytes 29360128 | tf_op args[0]
  51.6 27.0 %scatter_fusion = bf16[13,64,448]{2,1,0:T(8,128)(2,1)S(1)} fusion(bf16[13,64,448]{2,1,0:T(8,128)(2,1)S(1)} %broadcast_in_dim.12, s32[256]{0:T(256)S(1)} %compare_select_fusion.2, bf16[256,64,448]{2,1,0:T(8,128)(2,1)} %copy.14), kind=kCustom, calls=%fused_computation.3 | custom fusion | bytes 44041216 | tf_op jit(solution)/shard_map/scatter | solution.py:40
  78.6 1.0 slice.133
  79.6 3.7 all-to-all-start
  83.3 1.4 constant_dynamic-update-slice_fusion.6
  84.8 2.5 copy.15
  87.3 0.1 copy.18
  87.4 0.2 reshape.102
  87.6 8.9 %copy.16 = bf16[256,64,64]{1,2,0:T(8,128)(2,1)} copy(bf16[256,64,64]{0,2,1:T(8,128)(2,1)} %bitcast.50) | data formatting | bytes 4194304 | tf_op jit(solution)/shard_map/reshape | solution.py:55
  96.5 0.5 broadcast_compare_fusion
  97.1 14.4 %pad_maximum_fusion = bf16[268,64,448]{2,1,0:T(8,128)(2,1)} fusion(bf16[12,64,448]{2,1,0:T(8,128)(2,1)S(1)} %all-to-all-done, bf16[256,64,448]{2,1,0:T(8,128)(2,1)} %copy.14), kind=kLoop, calls=%fused_computation.4 | loop fusion | flops 7684096 | bytes 30736384 | tf_op jit(solution)/shard_map/concatenate | solution.py:44
  111.4 15.8 %gather_fusion = bf16[256,64,448]{2,1,0:T(8,128)(2,1)} fusion(bf16[268,64,448]{2,1,0:T(8,128)(2,1)} %pad_maximum_fusion, s32[1024]{0:T(1024)S(1)} %pad_clamp_fusion.2), kind=kCustom, calls=%fused_computation | custom fusion | bytes 29361152 | tf_op jit(solution)/shard_map/gather | solution.py:45
  127.2 12.9 %convert_bitcast_fusion = bf16[256,64,448]{2,1,0:T(8,128)(2,1)} fusion(bf16[256,64,64]{1,2,0:T(8,128)(2,1)} %copy.16, bf16[256,64,448]{2,1,0:T(8,128)(2,1)} %gather_fusion), kind=kOutput, calls=%fused_computation.5 | convolution fusion | flops 946864128 | bytes 31457280 | tf_op jit(solution)/shard_map/rba,rbx->rax/dot_general | solution.py:56
  140.1 23.6 %copy.17 = bf16[256,64,448]{0,2,1:T(8,128)(2,1)} copy(bf16[256,64,448]{2,1,0:T(8,128)(2,1)} %convert_bitcast_fusion) | data formatting | bytes 29360128 | tf_op jit(solution)/shard_map/convert_element_type | solution.py:58
  163.7 40.7 %copy.19 = bf16[256,64,7,64]{3,1,2,0:T(8,128)(2,1)} copy(bf16[256,64,7,64]{0,3,2,1:T(8,128)(2,1)} %bitcast.49) | data formatting | bytes 29360128 | tf_op jit(solution)/shard_map/reshape | solution.py:59
  204.5 3.7 collective-permute-start.11
  208.2 1.9 constant_dynamic-update-slice_fusion.5
  210.1 1.9 constant_dynamic-update-slice_fusion.4
  212.0 1.9 constant_dynamic-update-slice_fusion.3
  213.9 1.9 constant_dynamic-update-slice_fusion.2
  215.7 0.8 constant_dynamic-update-slice_fusion.1
  216.6 2.1 collective-permute-done.11
  218.7 0.8 constant_dynamic-update-slice_fusion
  219.5 28.8 %gather_fusion.2 = bf16[1792,4096]{1,0:T(8,128)(2,1)} fusion(bf16[640,4096]{1,0:T(8,128)(2,1)} %constant_dynamic-update-slice_fusion, s32[2048]{0:T(1024)S(1)} %pad_clamp_fusion), kind=kCustom, calls=%fused_computation.2 | custom fusion | bytes 29367296 | tf_op jit(solution)/shard_map/gather | solution.py:60
  248.3 40.3 %reshape.82 = bf16[256,7,64,64]{3,2,1,0:T(8,128)(2,1)} reshape(bf16[1792,4096]{1,0:T(8,128)(2,1)} %gather_fusion.2) | data formatting | bytes 29360128 | tf_op jit(solution)/shard_map/reshape | solution.py:60
  288.6 38.2 %fusion.13 = f32[256,7,64,64]{3,2,1,0:T(8,128)} fusion(bf16[256,64,7,64]{3,1,2,0:T(8,128)(2,1)} %copy.19, bf16[256,7,64,64]{3,2,1,0:T(8,128)(2,1)} %reshape.82), kind=kOutput, calls=%fused_computation.58 | convolution fusion | flops 939524096 | bytes 58720256 | tf_op jit(solution)/shard_map/rakb,rkbc->rkac/dot_general | solution.py:61
  326.8 45.8 %copy.20 = f32[256,7,64,64]{0,3,2,1:T(8,128)} copy(f32[256,7,64,64]{3,2,1,0:T(8,128)} %fusion.13) | data formatting | bytes 58720256 | tf_op jit(solution)/shard_map/rakb,rkbc->rkac/dot_general | solution.py:61
  372.6 19.8 %convolution_bitcast_fusion = f32[224,4096]{1,0:T(8,128)S(1)} fusion(f32[256,7,4096]{0,2,1:T(8,128)} %bitcast.48, s32[256,7]{0,1:T(8,128)S(1)} %copy-done.5, pred[256,7]{0,1:T(8,128)(4,1)S(1)} %copy-done.6), kind=kOutput, calls=%fused_computation.6 | convolution fusion | flops 19730808832 | bytes 33039104 | tf_op jit(solution)/shard_map/rku,rkx->ux/dot_general | solution.py:68
  392.5 1.3 fusion.11
  393.8 4.2 collective-permute-start.12
  398.0 1.3 collective-permute-start.13
  399.4 4.5 collective-permute-start
  403.9 1.3 collective-permute-start.1
  405.2 2.7 collective-permute-start.2
  407.9 1.1 collective-permute-done
  409.0 2.9 collective-permute-start.3
  411.9 2.6 collective-permute-done.1
  414.5 2.2 collective-permute-start.4
  416.7 4.3 collective-permute-start.5
  421.0 1.3 collective-permute-done.5
  422.3 1.9 collective-permute-start.14
  424.2 3.6 collective-permute-start.15
  427.9 3.3 collective-permute-start.16
  431.2 3.2 collective-permute-start.17
  434.4 1.9 constant_dynamic-update-slice_fusion.12
  436.2 1.9 constant_dynamic-update-slice_fusion.11
  438.1 0.8 constant_dynamic-update-slice_fusion.10
  439.0 0.8 constant_dynamic-update-slice_fusion.9
  439.8 9.3 %collective-permute-done.16 = f32[32,4096]{1,0:T(8,128)S(1)} collective-permute-done((f32[32,4096]{1,0:T(8,128)S(1)}, f32[32,4096]{1,0:T(8,128)S(1)}, u32[]{:S(2)}, u32[]{:S(2)}) %collective-permute-start.16) | collective-permute-done | bytes 524320 | tf_op jit(solution)/shard_map/ppermute | solution.py:18
  449.1 0.8 constant_dynamic-update-slice_fusion.8
  450.0 6.5 %collective-permute-done.17 = f32[32,4096]{1,0:T(8,128)S(1)} collective-permute-done((f32[32,4096]{1,0:T(8,128)S(1)}, f32[32,4096]{1,0:T(8,128)S(1)}, u32[]{:S(2)}, u32[]{:S(2)}) %collective-permute-start.17) | collective-permute-done | bytes 524320 | tf_op jit(solution)/shard_map/ppermute | solution.py:18
  456.5 0.9 constant_dynamic-update-slice_fusion.7
  457.4 4.6 fusion.4
  (45 shorter events, 0.6 us)
Async XLA Ops:
  10.2 16.8 %copy-start.4 = (s32[256]{0:T(256)S(1)}, s32[256]{0:T(256)}, u32[]{:S(2)}) copy-start(s32[256]{0:T(256)} %param.10) | copy-start | bytes 3076
  11.9 192.6 %collective-permute-start.6 = (bf16[64,4096]{1,0:T(8,128)(2,1)}, bf16[64,4096]{1,0:T(8,128)(2,1)}, u32[]{:S(2)}, u32[]{:S(2)}) collective-permute-start(bf16[64,4096]{1,0:T(8,128)(2,1)} %get-tuple-element.17), channel_id=1, source_target_pairs={{8,0},{9,1},{10,2},{11,3},{12,4},{13,5},{14,6},{15,7},{16,8},{17,9... | collective-permute-start | bytes 1572872 | tf_op jit(solution)/shard_map/ppermute | solution.py:18
  13.2 196.9 %collective-permute-start.7 = (bf16[64,4096]{1,0:T(8,128)(2,1)}, bf16[64,4096]{1,0:T(8,128)(2,1)}, u32[]{:S(2)}, u32[]{:S(2)}) collective-permute-start(bf16[64,4096]{1,0:T(8,128)(2,1)} %get-tuple-element.16), channel_id=1, source_target_pairs={{0,8},{1,9},{2,10},{3,11},{4,12},{5,13},{6,14},{7,15},{8,16},{9,17... | collective-permute-start | bytes 1572872 | tf_op jit(solution)/shard_map/ppermute | solution.py:18
  18.5 193.4 %collective-permute-start.8 = (bf16[64,4096]{1,0:T(8,128)(2,1)}, bf16[64,4096]{1,0:T(8,128)(2,1)}, u32[]{:S(2)}, u32[]{:S(2)}) collective-permute-start(bf16[64,4096]{1,0:T(8,128)(2,1)} %get-tuple-element.15), channel_id=1, source_target_pairs={{2,0},{3,1},{4,2},{5,3},{6,4},{7,5},{8,6},{9,7},{10,8},{11,9},{12,... | collective-permute-start | bytes 1572872 | tf_op jit(solution)/shard_map/ppermute | solution.py:18
  20.5 193.4 %collective-permute-start.9 = (bf16[64,4096]{1,0:T(8,128)(2,1)}, bf16[64,4096]{1,0:T(8,128)(2,1)}, u32[]{:S(2)}, u32[]{:S(2)}) collective-permute-start(bf16[64,4096]{1,0:T(8,128)(2,1)} %get-tuple-element.14), channel_id=1, source_target_pairs={{0,2},{1,3},{2,4},{3,5},{4,6},{5,7},{6,8},{7,9},{8,10},{9,11},{10,... | collective-permute-start | bytes 1572872 | tf_op jit(solution)/shard_map/ppermute | solution.py:18
  22.9 192.9 %collective-permute-start.10 = (bf16[64,4096]{1,0:T(8,128)(2,1)}, bf16[64,4096]{1,0:T(8,128)(2,1)S(1)}, u32[]{:S(2)}, u32[]{:S(2)}) collective-permute-start(bf16[64,4096]{1,0:T(8,128)(2,1)} %get-tuple-element.13), channel_id=1, source_target_pairs={{1,0},{2,1},{3,2},{4,3},{5,4},{6,5},{7,6},{8,7},{9,8},{10,9},{11,1... | collective-permute-start | bytes 1572872 | tf_op jit(solution)/shard_map/ppermute | solution.py:18
  51.6 31.7 %copy-start = (bf16[256,4096]{1,0:T(8,128)(2,1)S(1)}, bf16[256,4096]{1,0:T(8,128)(2,1)}, u32[]{:S(2)}) copy-start(bf16[256,4096]{1,0:T(8,128)(2,1)} %param.9) | copy-start | bytes 6291460
  78.6 6.2 %copy-start.2 = (s32[256,7]{0,1:T(8,128)S(1)}, s32[256,7]{0,1:T(8,128)}, u32[]{:S(2)}) copy-start(s32[256,7]{0,1:T(8,128)} %param.12) | copy-start | bytes 21508
  78.6 6.2 %copy-start.7 = (s32[256]{0:T(256)S(1)}, s32[256]{0:T(256)}, u32[]{:S(2)}) copy-start(s32[256]{0:T(256)} %param.11) | copy-start | bytes 3076
  79.6 17.5 %all-to-all-start = ((bf16[12,64,448]{2,1,0:T(8,128)(2,1)}), bf16[12,64,448]{2,1,0:T(8,128)(2,1)S(1)}, u32[]{:S(2)}, u32[]{:S(2)}) async-start(bf16[12,64,448]{2,1,0:T(8,128)(2,1)} %slice.133), calls=%async_computation | async-start | bytes 1572864 | tf_op jit(solution)/shard_map/all_to_all | solution.py:41
  163.7 40.7 %copy-start.1 = (bf16[64,4096]{1,0:T(8,128)(2,1)S(1)}, bf16[64,4096]{1,0:T(8,128)(2,1)}, u32[]{:S(2)}) copy-start(bf16[64,4096]{1,0:T(8,128)(2,1)} %get-tuple-element.12) | copy-start | bytes 1572868
  204.5 14.2 %collective-permute-start.11 = (bf16[64,4096]{1,0:T(8,128)(2,1)S(1)}, bf16[64,4096]{1,0:T(8,128)(2,1)S(1)}, u32[]{:S(2)}, u32[]{:S(2)}) collective-permute-start(bf16[64,4096]{1,0:T(8,128)(2,1)S(1)} %copy-done.1), channel_id=1, source_target_pairs={{0,1},{1,2},{2,3},{3,4},{4,5},{5,6},{6,7},{7,8},{8,9},{9,10},{10,1... | collective-permute-start | bytes 1572872 | tf_op jit(solution)/shard_map/ppermute | solution.py:18
  326.8 45.8 %copy-start.5 = (s32[256,7]{0,1:T(8,128)S(1)}, s32[256,7]{0,1:T(8,128)}, u32[]{:S(2)}) copy-start(s32[256,7]{0,1:T(8,128)} %param.13) | copy-start | bytes 21508
  326.8 45.8 %copy-start.6 = (pred[256,7]{0,1:T(8,128)(4,1)S(1)}, pred[256,7]{0,1:T(8,128)(4,1)}, u32[]{:S(2)}) copy-start(pred[256,7]{0,1:T(8,128)(4,1)} %broadcast_compare_fusion) | copy-start | bytes 5380
  392.4 6.8 %copy-start.3 = (s32[1,224]{1,0:T(1,128)S(1)}, s32[1,224]{1,0:T(1,128)}, u32[]{:S(2)}) copy-start(s32[1,224]{1,0:T(1,128)} %param.15) | copy-start | bytes 2692
  393.8 37.5 %collective-permute-start.12 = (f32[32,4096]{1,0:T(8,128)}, f32[32,4096]{1,0:T(8,128)}, u32[]{:S(2)}, u32[]{:S(2)}) collective-permute-start(f32[32,4096]{1,0:T(8,128)} %get-tuple-element.10), channel_id=1, source_target_pairs={{0,8},{1,9},{2,10},{3,11},{4,12},{5,13},{6,14},{7,15},{8,16},{9,17... | collective-permute-start | bytes 1572872 | tf_op jit(solution)/shard_map/ppermute | solution.py:18
  398.0 38.3 %collective-permute-start.13 = (f32[32,4096]{1,0:T(8,128)S(1)}, f32[32,4096]{1,0:T(8,128)}, u32[]{:S(2)}, u32[]{:S(2)}) collective-permute-start(f32[32,4096]{1,0:T(8,128)S(1)} %get-tuple-element.9), channel_id=1, source_target_pairs={{8,0},{9,1},{10,2},{11,3},{12,4},{13,5},{14,6},{15,7},{16,8},{17,9... | collective-permute-start | bytes 1572872 | tf_op jit(solution)/shard_map/ppermute | solution.py:18
  399.4 9.6 %collective-permute-start = (s32[32]{0:T(128)S(1)}, s32[32]{0:T(128)S(1)}, u32[]{:S(2)}, u32[]{:S(2)}) collective-permute-start(s32[32]{0:T(128)S(1)} %get-tuple-element.22), channel_id=1, source_target_pairs={{0,8},{1,9},{2,10},{3,11},{4,12},{5,13},{6,14},{7,15},{8,16},{9,17... | collective-permute-start | bytes 392 | tf_op jit(solution)/shard_map/ppermute | solution.py:18
  403.9 10.6 %collective-permute-start.1 = (s32[32]{0:T(128)S(1)}, s32[32]{0:T(128)S(1)}, u32[]{:S(2)}, u32[]{:S(2)}) collective-permute-start(s32[32]{0:T(128)S(1)} %get-tuple-element.21), channel_id=1, source_target_pairs={{8,0},{9,1},{10,2},{11,3},{12,4},{13,5},{14,6},{15,7},{16,8},{17,9... | collective-permute-start | bytes 392 | tf_op jit(solution)/shard_map/ppermute | solution.py:18
  405.2 11.5 %collective-permute-start.2 = (s32[32]{0:T(128)S(1)}, s32[32]{0:T(128)S(1)}, u32[]{:S(2)}, u32[]{:S(2)}) collective-permute-start(s32[32]{0:T(128)S(1)} %get-tuple-element.20), channel_id=1, source_target_pairs={{0,2},{1,3},{2,4},{3,5},{4,6},{5,7},{6,8},{7,9},{8,10},{9,11},{10,... | collective-permute-start | bytes 392 | tf_op jit(solution)/shard_map/ppermute | solution.py:18
  409.0 12.0 %collective-permute-start.3 = (s32[32]{0:T(128)S(1)}, s32[32]{0:T(128)S(1)}, u32[]{:S(2)}, u32[]{:S(2)}) collective-permute-start(s32[32]{0:T(128)S(1)} %get-tuple-element.19), channel_id=1, source_target_pairs={{2,0},{3,1},{4,2},{5,3},{6,4},{7,5},{8,6},{9,7},{10,8},{11,9},{12,... | collective-permute-start | bytes 392 | tf_op jit(solution)/shard_map/ppermute | solution.py:18
  414.5 6.5 %collective-permute-start.4 = (s32[32]{0:T(128)S(1)}, s32[32]{0:T(128)S(1)}, u32[]{:S(2)}, u32[]{:S(2)}) collective-permute-start(s32[32]{0:T(128)S(1)} %get-tuple-element.24), channel_id=1, source_target_pairs={{0,1},{1,2},{2,3},{3,4},{4,5},{5,6},{6,7},{7,8},{8,9},{9,10},{10,1... | collective-permute-start | bytes 392 | tf_op jit(solution)/shard_map/ppermute | solution.py:18
  416.7 5.5 %collective-permute-start.5 = (s32[32]{0:T(128)S(1)}, s32[32]{0:T(128)S(1)}, u32[]{:S(2)}, u32[]{:S(2)}) collective-permute-start(s32[32]{0:T(128)S(1)} %get-tuple-element.18), channel_id=1, source_target_pairs={{1,0},{2,1},{3,2},{4,3},{5,4},{6,5},{7,6},{8,7},{9,8},{10,9},{11,1... | collective-permute-start | bytes 392 | tf_op jit(solution)/shard_map/ppermute | solution.py:18
  422.3 15.8 %collective-permute-start.14 = (f32[32,4096]{1,0:T(8,128)S(1)}, f32[32,4096]{1,0:T(8,128)S(1)}, u32[]{:S(2)}, u32[]{:S(2)}) collective-permute-start(f32[32,4096]{1,0:T(8,128)S(1)} %get-tuple-element.8), channel_id=1, source_target_pairs={{0,2},{1,3},{2,4},{3,5},{4,6},{5,7},{6,8},{7,9},{8,10},{9,11},{10,... | collective-permute-start | bytes 1572872 | tf_op jit(solution)/shard_map/ppermute | solution.py:18
  424.2 14.7 %collective-permute-start.15 = (f32[32,4096]{1,0:T(8,128)S(1)}, f32[32,4096]{1,0:T(8,128)S(1)}, u32[]{:S(2)}, u32[]{:S(2)}) collective-permute-start(f32[32,4096]{1,0:T(8,128)S(1)} %get-tuple-element.7), channel_id=1, source_target_pairs={{2,0},{3,1},{4,2},{5,3},{6,4},{7,5},{8,6},{9,7},{10,8},{11,9},{12,... | collective-permute-start | bytes 1572872 | tf_op jit(solution)/shard_map/ppermute | solution.py:18
  427.9 21.2 %collective-permute-start.16 = (f32[32,4096]{1,0:T(8,128)S(1)}, f32[32,4096]{1,0:T(8,128)S(1)}, u32[]{:S(2)}, u32[]{:S(2)}) collective-permute-start(f32[32,4096]{1,0:T(8,128)S(1)} %get-tuple-element.6), channel_id=1, source_target_pairs={{0,1},{1,2},{2,3},{3,4},{4,5},{5,6},{6,7},{7,8},{8,9},{9,10},{10,1... | collective-permute-start | bytes 1572872 | tf_op jit(solution)/shard_map/ppermute | solution.py:18
  431.2 25.3 %collective-permute-start.17 = (f32[32,4096]{1,0:T(8,128)S(1)}, f32[32,4096]{1,0:T(8,128)S(1)}, u32[]{:S(2)}, u32[]{:S(2)}) collective-permute-start(f32[32,4096]{1,0:T(8,128)S(1)} %get-tuple-element.5), channel_id=1, source_target_pairs={{1,0},{2,1},{3,2},{4,3},{5,4},{6,5},{7,6},{8,7},{9,8},{10,9},{11,1... | collective-permute-start | bytes 1572872 | tf_op jit(solution)/shard_map/ppermute | solution.py:18
where the time goes:
time: 467 us; the launch traced here: 462 us
  local copies, waits for them, and re-layouts  289 us (62%)
  matrix products  75.4 us (16%)
  starting transfers between devices  57.9 us (12%)
  waiting for transfers between devices  22.9 us (5%)
  other arithmetic  16.6 us (4%)
    ppermute x18, starting transfers between devices, shifted(): return lax.ppermute(value, axis, pairs)  54.2 us
    dot_general x1, local copies, waits for them, and re-layouts, shards(): jnp.einsum('rakb,rkbc->rkac', left, neighbour, preferred_element_type=jnp...  45.8 us
    unnamed x29, local copies, waits for them, and re-layouts  41.9 us
    reshape x1, local copies, waits for them, and re-layouts, shards(): left = left.reshape(row_count, block_side, NBR, block_side)  40.7 us
    reshape x1, local copies, waits for them, and re-layouts, shards(): block_table[jnp.maximum(columns, 0)]  40.3 us
    dot_general x1, matrix products, shards(): jnp.einsum('rakb,rkbc->rkac', left, neighbour, preferred_element_type=jnp...  38.2 us
    gather x1, local copies, waits for them, and re-layouts, shards(): block_table[jnp.maximum(columns, 0)]  28.8 us
    scatter x1, local copies, waits for them, and re-layouts, shards(): jnp.zeros((layers * CAP + 1,) + row_shape, jnp.bfloat16).at[slot_key]  27 us
  transfers between devices with their start and end apart: 19, of which 6 were waited for; matrix products, arithmetic and copies ran while one was open for 41% of the time, Pallas kernels for 0%

commit v1 on v0

v1 whole, which is shorter than its diff:
```python
import functools

import jax
import jax.numpy as jnp
from jax import lax
from jax.experimental import pallas as pl
from jax.experimental.pallas import tpu as pltpu
from jax.sharding import PartitionSpec as P

B = 64
NBR = 7
CAP = 6
AXES = ("gx", "gy", "gz")
FACES = 6
MESH = pl.DeviceIdType.MESH
VMEM_LIMIT = 60 * 1024 * 1024
ROW_CHUNKS = 8
ANY = pl.BlockSpec(memory_space=pl.ANY)
VMEM = pl.BlockSpec(memory_space=pltpu.VMEM)
SMEM = pl.BlockSpec(memory_space=pltpu.SMEM)


def face(direction):
    axis = AXES[direction // 2]
    there = lax.axis_index(axis) + (1 - 2 * (direction % 2))
    inside = (there >= 0) & (there < lax.axis_size(axis))
    return axis, there, inside


def pick_rows(index_ref, blocks_ref, out_ref, sems):
    copies = [
        pltpu.make_async_copy(blocks_ref.at[index_ref[s]], out_ref.at[s], sems.at[s])
        for s in range(out_ref.shape[0])
    ]
    for copy in copies:
        copy.start()
    for copy in copies:
        copy.wait()


def exchange_first(
    lists_ref, own_ref, leaving_ref, numbers_ref, ghost_ref, arriving_ref, got_ref,
    outbound, send_sem, recv_sem, num_send, num_recv, row_send, row_recv,
):
    layers = lax.axis_size("gz")
    layer = lax.axis_index("gz")
    barrier = pltpu.get_barrier_semaphore()
    expected = layers - 1
    for direction in range(4):
        axis, there, inside = face(direction)
        expected = expected + inside.astype(jnp.int32)

        @pl.when(inside)
        def _():
            pl.semaphore_signal(barrier, inc=1, device_id={axis: there}, device_id_type=MESH)

    for step in range(1, layers):
        pl.semaphore_signal(
            barrier, inc=1, device_id={"gz": lax.rem(layer + step, layers)}, device_id_type=MESH
        )
    pl.semaphore_wait(barrier, expected)

    def row_copy(step):
        target = lax.rem(layer + step, layers)
        return pltpu.make_async_remote_copy(
            src_ref=leaving_ref.at[pl.ds(target * CAP, CAP)],
            dst_ref=arriving_ref.at[pl.ds(layer * CAP, CAP)],
            send_sem=row_send.at[step - 1],
            recv_sem=row_recv.at[step - 1],
            device_id={"gz": target},
            device_id_type=MESH,
        )

    def ghost_copy(direction, axis, there):
        return pltpu.make_async_remote_copy(
            src_ref=outbound.at[direction],
            dst_ref=ghost_ref.at[direction ^ 1],
            send_sem=send_sem.at[direction],
            recv_sem=recv_sem.at[direction ^ 1],
            device_id={axis: there},
            device_id_type=MESH,
        )

    def number_copy(direction, axis, there):
        return pltpu.make_async_remote_copy(
            src_ref=numbers_ref.at[direction],
            dst_ref=got_ref.at[direction ^ 1],
            send_sem=num_send.at[direction],
            recv_sem=num_recv.at[direction ^ 1],
            device_id={axis: there},
            device_id_type=MESH,
        )

    for step in range(1, layers):
        row_copy(step).start()
    count = outbound.shape[1]
    for direction in (4, 5, 0, 1, 2, 3):

        def gather(q, carry, direction=direction):
            outbound[direction, q] = own_ref[lists_ref[direction * count + q]]
            return carry

        lax.fori_loop(0, count, gather, 0, unroll=8)
        axis, there, inside = face(direction)

        @pl.when(inside)
        def _():
            ghost_copy(direction, axis, there).start()
            number_copy(direction, axis, there).start()

    for direction in range(FACES):
        axis, there, inside = face(direction)

        @pl.when(inside)
        def _():
            ghost_copy(direction, axis, there).wait_send()
            number_copy(direction, axis, there).wait_send()
            ghost_copy(direction ^ 1, axis, there).wait_recv()
            number_copy(direction ^ 1, axis, there).wait_recv()

    for step in range(1, layers):
        row_copy(step).wait()


def product(
    arrival_ref, column_ref, target_ref, own_ref, ghost_ref, order_ref, blocks_ref, arriving_ref,
    kept_ref, sent_ref, table, rows, sum_a, sum_b, sems,
):
    row_count = rows.shape[0]
    chunk = row_count // ROW_CHUNKS

    def fetch(n, carry):
        a = arrival_ref[n]

        @pl.when(a < row_count)
        def _():
            pltpu.make_async_copy(blocks_ref.at[a], rows.at[n], sems.at[n // chunk]).start()

        @pl.when(a >= row_count)
        def _():
            pltpu.make_async_copy(
                arriving_ref.at[a - row_count], rows.at[n], sems.at[n // chunk]
            ).start()

        return carry

    lax.fori_loop(0, row_count, fetch, 0)
    low = lax.broadcasted_iota(jnp.int32, (B // 2, 2 * B), 1) < B
    low_full = lax.broadcasted_iota(jnp.int32, (B, 2 * B), 1) < B
    order = order_ref[...]

    def clear(u, carry):
        sum_a[u] = jnp.zeros(sum_a.shape[1:], jnp.float32)
        sum_b[u] = jnp.zeros(sum_b.shape[1:], jnp.float32)
        return carry

    lax.fori_loop(0, sum_a.shape[0], clear, 0, unroll=2)

    def unfold(source, base):
        def body(g, carry):
            parts = []
            for j in range(4):
                paired = source[4 * g + j].astype(jnp.float32)
                turned = pltpu.roll(paired, B, 1)
                parts.append(
                    jnp.concatenate(
                        [jnp.where(low, paired, turned), jnp.where(low, turned, paired)], axis=0
                    ).astype(jnp.bfloat16)
                )
            full = jnp.dot(
                order, jnp.concatenate(parts, axis=1), preferred_element_type=jnp.float32
            ).astype(jnp.bfloat16)
            for j in range(4):
                table[base + 4 * g + j] = full[:, 2 * B * j : 2 * B * (j + 1)]
            return carry

        lax.fori_loop(0, source.shape[0] // 4, body, 0, unroll=2)

    unfold(own_ref, 0)
    unfold(ghost_ref, row_count)
    table[table.shape[0] - 1] = jnp.zeros(table.shape[1:], jnp.bfloat16)
    zero = jnp.zeros((B, 2 * B), jnp.bfloat16)

    def one_row(n):
        left = lax.dot_general(
            table[n, :, :B], rows[n], (((0,), (0,)), ((), ())), preferred_element_type=jnp.float32
        ).astype(jnp.bfloat16)
        found = []
        for pair in range(NBR // 2):
            k = 2 * pair
            first = jnp.where(low_full, table[column_ref[n * NBR + k]], zero)
            second = jnp.where(low_full, zero, table[column_ref[n * NBR + k + 1]])
            found.append(
                jnp.dot(
                    left[:, B * k : B * (k + 2)],
                    jnp.concatenate([first, second], axis=0),
                    preferred_element_type=jnp.float32,
                )
            )
        k = NBR - 1
        found.append(
            jnp.dot(
                left[:, B * k :], table[column_ref[n * NBR + k]], preferred_element_type=jnp.float32
            )
        )
        for k in range(NBR):
            sums = (sum_a, sum_b)[k // 2 % 2]
            u = target_ref[n * NBR + k]
            half = slice(B * (k % 2), B * (k % 2 + 1))
            sums[u, :, half] = sums[u, :, half] + found[k // 2][:, half]

    def some_rows(c, carry):
        whole = rows.at[pl.ds(c * chunk, chunk)]
        pltpu.make_async_copy(whole, whole, sems.at[c]).wait()

        def body(i, inner):
            one_row(c * chunk + 2 * i)
            one_row(c * chunk + 2 * i + 1)
            return inner

        return lax.fori_loop(0, chunk // 2, body, carry)

    lax.fori_loop(0, ROW_CHUNKS, some_rows, 0)

    def folded(u):
        even = sum_a[u, pl.ds(0, B // 2, stride=2)] + sum_b[u, pl.ds(0, B // 2, stride=2)]
        odd = sum_a[u, pl.ds(1, B // 2, stride=2)] + sum_b[u, pl.ds(1, B // 2, stride=2)]
        return jnp.where(low, even + pltpu.roll(even, B, 1), odd + pltpu.roll(odd, B, 1))

    kept = kept_ref.shape[0]

    def keep(u, carry):
        kept_ref[u] = folded(u)
        return carry

    def hand_over(u, carry):
        sent_ref[u] = folded(u + kept).astype(jnp.bfloat16)
        return carry

    lax.fori_loop(0, kept, keep, 0, unroll=2)
    lax.fori_loop(0, sent_ref.shape[0], hand_over, 0, unroll=2)


def exchange_last(sent_ref, got_ref, send_sem, recv_sem):
    barrier = pltpu.get_barrier_semaphore()
    expected = 0
    for direction in range(FACES):
        axis, there, inside = face(direction)
        expected = expected + inside.astype(jnp.int32)

        @pl.when(inside)
        def _():
            pl.semaphore_signal(barrier, inc=1, device_id={axis: there}, device_id_type=MESH)

    pl.semaphore_wait(barrier, expected)

    def slot_copy(direction, axis, there):
        return pltpu.make_async_remote_copy(
            src_ref=sent_ref.at[direction],
            dst_ref=got_ref.at[direction ^ 1],
            send_sem=send_sem.at[direction],
            recv_sem=recv_sem.at[direction ^ 1],
            device_id={axis: there},
            device_id_type=MESH,
        )

    for direction in range(FACES):
        axis, there, inside = face(direction)

        @pl.when(inside)
        def _():
            slot_copy(direction, axis, there).start()

    for direction in range(FACES):
        axis, there, inside = face(direction)

        @pl.when(inside)
        def _():
            slot_copy(direction, axis, there).wait_send()
            slot_copy(direction ^ 1, axis, there).wait_recv()


def add_up(entry_ref, kept_ref, got_ref, coarse_ref, total):
    total[...] = jnp.zeros_like(total)
    kept = kept_ref.shape[0]

    def own(u, carry):
        e = entry_ref[u]
        total[e] = total[e] + kept_ref[u]
        return carry

    def other(u, carry):
        e = entry_ref[u + kept]
        total[e] = total[e] + got_ref[u].astype(jnp.float32)
        return carry

    lax.fori_loop(0, kept, own, 0, unroll=4)
    lax.fori_loop(0, got_ref.shape[0], other, 0, unroll=4)
    coarse_ref[...] = total[: coarse_ref.shape[0]]


def shards(entries, blocks, prolong, new_owner, arrival, columns, targets, ghost_lists, touched):
    row_count = blocks.shape[0]
    area = prolong.shape[1]
    layers = lax.axis_size("gz")
    layer = lax.axis_index("gz")
    ghosts = ghost_lists.shape[2]
    slots = touched.shape[1]
    share = slots // (FACES + 1)
    paired = (area // (2 * B), 2 * B)
    any_kernel = dict(vmem_limit_bytes=VMEM_LIMIT)

    peer = new_owner % layers
    row_ids = jnp.arange(row_count, dtype=jnp.int32)
    before = (peer[:, None] == peer[None, :]) & (row_ids[:, None] < row_ids[None, :])
    rank = jnp.sum(before.astype(jnp.int32), axis=0)
    key = jnp.where(peer == layer, -1, peer * CAP + rank)
    slot_ids = jnp.arange(layers * CAP, dtype=jnp.int32)
    chosen = jnp.sum(jnp.where(key[:, None] == slot_ids[None, :], row_ids[:, None], 0), axis=0)
    leaving = pl.pallas_call(
        pick_rows,
        out_shape=jax.ShapeDtypeStruct((layers * CAP,) + blocks.shape[1:], blocks.dtype),
        in_specs=[SMEM, ANY],
        out_specs=ANY,
        scratch_shapes=[pltpu.SemaphoreType.DMA((layers * CAP,))],
        name="pick_rows",
    )(chosen.astype(jnp.int32), blocks)

    own = prolong.reshape((row_count,) + paired)
    numbers = jnp.pad(touched.reshape(FACES + 1, 1, share)[1:], ((0, 0), (0, 7), (0, 128 - share)))
    ghost, arriving, got_numbers = pl.pallas_call(
        exchange_first,
        out_shape=[
            jax.ShapeDtypeStruct((FACES, ghosts) + paired, prolong.dtype),
            jax.ShapeDtypeStruct(leaving.shape, blocks.dtype),
            jax.ShapeDtypeStruct(numbers.shape, jnp.int32),
        ],
        in_specs=[SMEM, VMEM, ANY, ANY],
        out_specs=[ANY, ANY, ANY],
        scratch_shapes=[pltpu.VMEM((FACES, ghosts) + paired, prolong.dtype)]
        + [pltpu.SemaphoreType.DMA((FACES,))] * 4
        + [pltpu.SemaphoreType.DMA((layers - 1,))] * 2,
        compiler_params=pltpu.CompilerParams(
            collective_id=0, has_side_effects=True, **any_kernel
        ),
        name="exchange_first",
    )(ghost_lists.reshape(-1), own, leaving, numbers)

    place = jnp.arange(B, dtype=jnp.int32)
    order = (
        place[None, :] == (place[:, None] % 2) * (B // 2) + place[:, None] // 2
    ).astype(jnp.bfloat16)
    table_size = row_count + FACES * ghosts
    where = jnp.where(columns < 0, table_size, columns).reshape(-1)
    kept, sent = pl.pallas_call(
        product,
        out_shape=[
            jax.ShapeDtypeStruct((share,) + paired, jnp.float32),
            jax.ShapeDtypeStruct((FACES * share,) + paired, jnp.bfloat16),
        ],
        in_specs=[SMEM, SMEM, SMEM, VMEM, VMEM, VMEM, ANY, ANY],
        out_specs=[VMEM, VMEM],
        scratch_shapes=[
            pltpu.VMEM((table_size + 1, B, 2 * B), jnp.bfloat16),
            pltpu.VMEM(blocks.shape, blocks.dtype),
            pltpu.VMEM((slots, B, 2 * B), jnp.float32),
            pltpu.VMEM((slots, B, 2 * B), jnp.float32),
            pltpu.SemaphoreType.DMA((ROW_CHUNKS,)),
        ],
        compiler_params=pltpu.CompilerParams(**any_kernel),
        name="product",
    )(
        arrival, where, targets.reshape(-1), own, ghost.reshape((FACES * ghosts,) + paired),
        order, blocks, arriving,
    )

    got = pl.pallas_call(
        exchange_last,
        out_shape=jax.ShapeDtypeStruct((FACES, share) + paired, jnp.bfloat16),
        in_specs=[ANY],
        out_specs=ANY,
        scratch_shapes=[pltpu.SemaphoreType.DMA((FACES,))] * 2,
        compiler_params=pltpu.CompilerParams(collective_id=1, has_side_effects=True),
        name="exchange_last",
    )(sent.reshape((FACES, share) + paired))

    there = jnp.stack([face(direction)[2] for direction in range(FACES)])
    got_entry = jnp.where(there[:, None], got_numbers[:, 0, :share], entries).reshape(-1)
    entry = jnp.concatenate([touched[0, :share], got_entry])
    coarse = pl.pallas_call(
        add_up,
        out_shape=jax.ShapeDtypeStruct((entries,) + paired, jnp.float32),
        in_specs=[SMEM, VMEM, VMEM],
        out_specs=VMEM,
        scratch_shapes=[pltpu.VMEM((entries + 1,) + paired, jnp.float32)],
        name="add_up",
    )(entry, kept, got.reshape((FACES * share,) + paired))
    return coarse.reshape(entries, area)


ENTRIES = 64


def solution(mesh):
    rows = P(AXES)
    in_specs = (
        P(AXES, None, None), P(AXES, None), rows, rows,
        P(AXES, None), P(AXES, None), P(AXES, None, None), P(AXES, None),
    )
    return jax.shard_map(
        functools.partial(shards, ENTRIES),
        mesh=mesh,
        in_specs=in_specs,
        out_specs=P(AXES, None),
        check_vma=False,
    )
```

time: 467 us -> 208 us (0.45)
  the two profiles are of different devices: /device:TPU:2 before, /device:TPU:0 now
where the time goes in v1:
time: 208 us; the launch traced here: 207 us
  Pallas kernels  166 us (80%)
  local copies, waits for them, and re-layouts  36 us (17%)
  other arithmetic  4.82 us (2%)
    pallas_call x1, Pallas kernels, shards(): pl.pallas_call(product, out_shape=[jax.ShapeDtypeStruct((share,) + paired...  99.4 us
    unnamed x4, local copies, waits for them, and re-layouts  30.4 us
    pallas_call x1, Pallas kernels, shards(): pl.pallas_call(exchange_first, out_shape=[jax.ShapeDtypeStruct((FACES, gh...  27.4 us
    pallas_call x1, Pallas kernels, shards(): pl.pallas_call(pick_rows, out_shape=jax.ShapeDtypeStruct((layers * CAP,)...  25.7 us
    pallas_call x1, Pallas kernels, shards(): pl.pallas_call(exchange_last, out_shape=jax.ShapeDtypeStruct((FACES, shar...  9.66 us

profile of v1, /device:TPU:0, one launch (start us, length us, event | category | flops | bytes accessed | tf_op | source)
XLA Modules:
  0.0 206.9 jit_solution(15352243513819208989)
XLA Ops:
  0.0 0.1 stack.27
  0.1 0.7 slice_bitcast_fusion
  0.8 0.1 broadcast_in_dim.45
  0.8 0.1 broadcast_in_dim.46
  0.9 0.7 and_select_fusion.2
  1.6 0.1 convert_reduce_fusion
  1.7 0.7 compare_select_fusion.3
  2.4 0.6 select_reduce_fusion.index_ref
  3.1 0.8 slice_reduce_fusion.1
  3.8 0.1 slice.14
  3.9 0.7 reduce
  4.6 0.6 reshape.88.lists_ref
  5.3 0.7 compare_select_fusion
  6.0 0.7 fusion.1.order_ref
  6.6 0.6 pad.4.numbers_ref
  7.2 0.1 copy.16
  7.4 0.8 reshape.90.column_ref
  8.2 0.8 copy.17
  9.0 0.8 reshape.91.target_ref
  9.8 3.4 %copy.19 = bf16[32,8,32,128]{3,2,1,0:T(8,128)(2,1)} copy(bf16[32,8,32,128]{3,1,2,0:T(8,128)(2,1)} %bitcast.22) | data formatting | bytes 4194304
  13.3 23.3 %copy.15.blocks_ref = bf16[256,64,448]{2,1,0:T(8,128)(2,1)} copy(bf16[256,64,448]{0,2,1:T(8,128)(2,1)} %param.8) | data formatting | bytes 29360128 | tf_op args[0]
  36.6 25.7 %pick_rows.1.leaving_ref = bf16[12,64,448]{2,1,0:T(8,128)(2,1)} custom-call(s32[12]{0:T(128)} %select_reduce_fusion.index_ref, bf16[256,64,448]{2,1,0:T(8,128)(2,1)} %copy.15.blocks_ref), custom_call_target="tpu_custom_call" | custom-call | tf_op jit(solution)/shard_map/pick_rows/pallas_call | solution.py:320
  62.3 27.4 %exchange_first.1 = (bf16[6,64,32,128]{3,2,1,0:T(8,128)(2,1)}, bf16[12,64,448]{2,1,0:T(8,128)(2,1)}, s32[6,8,128]{2,1,0:T(8,128)}) custom-call(s32[384]{0:T(512)} %reshape.88.lists_ref, bf16[256,32,128]{2,1,0:T(8,128)(2,1)} %bitcast.17, bf16[12,64,448]{2,1,0:T(8,128)(2,1)} %pick_rows.1.leaving_ref, s32[6,8,128]{2,1,0:T(8,128)} %pad.4.numbers_ref), custom_call_target="tpu_custom_call" | custom-call | tf_op jit(solution)/shard_map/exchange_first/pallas_call | solution.py:331
  89.7 0.8 slice_reduce_fusion
  90.4 0.1 squeeze.7
  90.5 0.6 pad_add_fusion.entry_ref
  91.1 99.4 %product.1 = (f32[32,32,128]{2,1,0:T(8,128)}, bf16[192,32,128]{2,1,0:T(8,128)(2,1)}) custom-call(s32[256]{0:T(256)} %arrival_ref.1, s32[1792]{0:T(1024)} %reshape.90.column_ref, s32[1792]{0:T(1024)} %reshape.91.target_ref, bf16[256,32,128]{2,1,0:T(8,128)(2,1)} %bitcast.18, bf16[384,32,128]{2,1,0:T(8,128)(2,1)} %bitcast.21, bf16[64,64]{1,0:T(8,128)(2,1)} %fusion.1.order_ref, ...), custom_call_target="tpu_custom_call" | custom-call | tf_op jit(solution)/shard_map/product/pallas_call | solution.py:355
  190.5 9.7 %exchange_last.1 = bf16[6,32,32,128]{3,2,1,0:T(8,128)(2,1)} custom-call(bf16[6,32,32,128]{3,2,1,0:T(8,128)(2,1)} %bitcast.23), custom_call_target="tpu_custom_call" | custom-call | tf_op jit(solution)/shard_map/exchange_last/pallas_call | solution.py:377
  200.2 3.9 %add_up.1 = f32[64,32,128]{2,1,0:T(8,128)} custom-call(s32[224]{0:T(256)} %pad_add_fusion.entry_ref, f32[32,32,128]{2,1,0:T(8,128)} %get-tuple-element.13.kept_ref, bf16[192,32,128]{2,1,0:T(8,128)(2,1)} %bitcast.19), custom_call_target="tpu_custom_call" | custom-call | tf_op jit(solution)/shard_map/add_up/pallas_call | solution.py:390
  204.1 2.8 %copy.22 = f32[8,8,32,128]{3,1,2,0:T(8,128)} copy(f32[8,8,32,128]{3,2,1,0:T(8,128)} %bitcast.20) | data formatting | bytes 2097152
  (2 shorter events, 0.0 us)

commit v2 on v1

--- a/solution.py
+++ b/solution.py
@@ -123,7 +123,7 @@
 
 
 def product(
-    arrival_ref, column_ref, target_ref, own_ref, ghost_ref, order_ref, blocks_ref, arriving_ref,
+    arrival_ref, column_ref, target_ref, own_ref, ghost_ref, blocks_ref, arriving_ref,
     kept_ref, sent_ref, table, rows, sum_a, sum_b, sems,
 ):
     row_count = rows.shape[0]
@@ -144,17 +144,21 @@
 
         return carry
 
-    lax.fori_loop(0, row_count, fetch, 0)
+    lax.fori_loop(0, row_count, fetch, 0, unroll=8)
     low = lax.broadcasted_iota(jnp.int32, (B // 2, 2 * B), 1) < B
     low_full = lax.broadcasted_iota(jnp.int32, (B, 2 * B), 1) < B
-    order = order_ref[...]
+    place = lax.broadcasted_iota(jnp.int32, (B, B), 0)
+    column = lax.broadcasted_iota(jnp.int32, (B, B), 1)
+    order = jnp.where(
+        column == (place & 1) * (B // 2) + (place >> 1), jnp.float32(1), jnp.float32(0)
+    ).astype(jnp.bfloat16)
 
     def clear(u, carry):
         sum_a[u] = jnp.zeros(sum_a.shape[1:], jnp.float32)
         sum_b[u] = jnp.zeros(sum_b.shape[1:], jnp.float32)
         return carry
 
-    lax.fori_loop(0, sum_a.shape[0], clear, 0, unroll=2)
+    lax.fori_loop(0, sum_a.shape[0], clear, 0, unroll=8)
 
     def unfold(source, base):
         def body(g, carry):
@@ -174,51 +178,61 @@
                 table[base + 4 * g + j] = full[:, 2 * B * j : 2 * B * (j + 1)]
             return carry
 
-        lax.fori_loop(0, source.shape[0] // 4, body, 0, unroll=2)
+        lax.fori_loop(0, source.shape[0] // 4, body, 0, unroll=8)
 
     unfold(own_ref, 0)
     unfold(ghost_ref, row_count)
     table[table.shape[0] - 1] = jnp.zeros(table.shape[1:], jnp.bfloat16)
     zero = jnp.zeros((B, 2 * B), jnp.bfloat16)
 
-    def one_row(n):
-        left = lax.dot_general(
-            table[n, :, :B], rows[n], (((0,), (0,)), ((), ())), preferred_element_type=jnp.float32
-        ).astype(jnp.bfloat16)
+    def entry(n, k):
+        c = column_ref[k, n]
+        return jnp.where(c < 0, table.shape[0] - 1, c)
+
+    def some_rows_at(first):
+        ns = [first + r for r in range(8)]
+        lefts = [
+            lax.dot_general(
+                table[n, :, :B], rows[n], (((0,), (0,)), ((), ())), preferred_element_type=jnp.float32
+            ).astype(jnp.bfloat16)
+            for n in ns
+        ]
         found = []
-        for pair in range(NBR // 2):
-            k = 2 * pair
-            first = jnp.where(low_full, table[column_ref[n * NBR + k]], zero)
-            second = jnp.where(low_full, zero, table[column_ref[n * NBR + k + 1]])
-            found.append(
-                jnp.dot(
-                    left[:, B * k : B * (k + 2)],
-                    jnp.concatenate([first, second], axis=0),
-                    preferred_element_type=jnp.float32,
+        for n, left in zip(ns, lefts):
+            mine = []
+            for k in range(0, NBR, 2):
+                if k + 1 < NBR:
+                    right = jnp.concatenate(
+                        [
+                            jnp.where(low_full, table[entry(n, k)], zero),
+                            jnp.where(low_full, zero, table[entry(n, k + 1)]),
+                        ],
+                        axis=0,
+                    )
+                else:
+                    right = table[entry(n, k)]
+                mine.append(
+                    jnp.dot(
+                        left[:, B * k : B * (k + 2)], right, preferred_element_type=jnp.float32
+                    )
                 )
-            )
-        k = NBR - 1
-        found.append(
-            jnp.dot(
-                left[:, B * k :], table[column_ref[n * NBR + k]], preferred_element_type=jnp.float32
-            )
-        )
-        for k in range(NBR):
-            sums = (sum_a, sum_b)[k // 2 % 2]
-            u = target_ref[n * NBR + k]
-            half = slice(B * (k % 2), B * (k % 2 + 1))
-            sums[u, :, half] = sums[u, :, half] + found[k // 2][:, half]
+            found.append(mine)
+        for n, mine in zip(ns, found):
+            for k in range(NBR):
+                sums = (sum_a, sum_b)[k // 2 % 2]
+                u = target_ref[k, n]
+                half = slice(B * (k % 2), B * (k % 2 + 1))
+                sums[u, :, half] = sums[u, :, half] + mine[k // 2][:, half]
 
     def some_rows(c, carry):
         whole = rows.at[pl.ds(c * chunk, chunk)]
         pltpu.make_async_copy(whole, whole, sems.at[c]).wait()
 
         def body(i, inner):
-            one_row(c * chunk + 2 * i)
-            one_row(c * chunk + 2 * i + 1)
+            some_rows_at(c * chunk + 8 * i)
             return inner
 
-        return lax.fori_loop(0, chunk // 2, body, carry)
+        return lax.fori_loop(0, chunk // 8, body, carry)
 
     lax.fori_loop(0, ROW_CHUNKS, some_rows, 0)
 
@@ -237,8 +251,8 @@
         sent_ref[u] = folded(u + kept).astype(jnp.bfloat16)
         return carry
 
-    lax.fori_loop(0, kept, keep, 0, unroll=2)
-    lax.fori_loop(0, sent_ref.shape[0], hand_over, 0, unroll=2)
+    lax.fori_loop(0, kept, keep, 0, unroll=8)
+    lax.fori_loop(0, sent_ref.shape[0], hand_over, 0, unroll=8)
 
 
 def exchange_last(sent_ref, got_ref, send_sem, recv_sem):
@@ -294,8 +308,8 @@
         total[e] = total[e] + got_ref[u].astype(jnp.float32)
         return carry
 
-    lax.fori_loop(0, kept, own, 0, unroll=4)
-    lax.fori_loop(0, got_ref.shape[0], other, 0, unroll=4)
+    lax.fori_loop(0, kept, own, 0, unroll=8)
+    lax.fori_loop(0, got_ref.shape[0], other, 0, unroll=8)
     coarse_ref[...] = total[: coarse_ref.shape[0]]
 
 
@@ -321,8 +335,9 @@
         pick_rows,
         out_shape=jax.ShapeDtypeStruct((layers * CAP,) + blocks.shape[1:], blocks.dtype),
         in_specs=[SMEM, ANY],
-        out_specs=ANY,
+        out_specs=VMEM,
         scratch_shapes=[pltpu.SemaphoreType.DMA((layers * CAP,))],
+        compiler_params=pltpu.CompilerParams(**any_kernel),
         name="pick_rows",
     )(chosen.astype(jnp.int32), blocks)
 
@@ -346,19 +361,14 @@
         name="exchange_first",
     )(ghost_lists.reshape(-1), own, leaving, numbers)
 
-    place = jnp.arange(B, dtype=jnp.int32)
-    order = (
-        place[None, :] == (place[:, None] % 2) * (B // 2) + place[:, None] // 2
-    ).astype(jnp.bfloat16)
     table_size = row_count + FACES * ghosts
-    where = jnp.where(columns < 0, table_size, columns).reshape(-1)
     kept, sent = pl.pallas_call(
         product,
         out_shape=[
             jax.ShapeDtypeStruct((share,) + paired, jnp.float32),
             jax.ShapeDtypeStruct((FACES * share,) + paired, jnp.bfloat16),
         ],
-        in_specs=[SMEM, SMEM, SMEM, VMEM, VMEM, VMEM, ANY, ANY],
+        in_specs=[SMEM, SMEM, SMEM, VMEM, VMEM, ANY, ANY],
         out_specs=[VMEM, VMEM],
         scratch_shapes=[
             pltpu.VMEM((table_size + 1, B, 2 * B), jnp.bfloat16),
@@ -370,8 +380,8 @@
         compiler_params=pltpu.CompilerParams(**any_kernel),
         name="product",
     )(
-        arrival, where, targets.reshape(-1), own, ghost.reshape((FACES * ghosts,) + paired),
-        order, blocks, arriving,
+        arrival, columns.T, targets.T, own, ghost.reshape((FACES * ghosts,) + paired),
+        blocks, arriving,
     )
 
     got = pl.pallas_call(

time: 208 us -> 118 us (0.57)
  Pallas kernels: 166 us -> 80.3 us
  local copies, waits for them, and re-layouts: 36 us -> 33.4 us
    pallas_call x1, Pallas kernels: 99.4 us -> 36.5 us  [shards(): pl.pallas_call(product, out_shape=[jax.ShapeDtypeStruct((share,) + paired...]
    pallas_call x1, Pallas kernels: 25.7 us -> 2.83 us  [shards(): pl.pallas_call(pick_rows, out_shape=jax.ShapeDtypeStruct((layers * CAP,)...]
    unnamed x4 -> x3, local copies, waits for them, and re-layouts: 30.4 us -> 29.6 us
where the time goes in v2:
time: 118 us; the launch traced here: 117 us
  Pallas kernels  80.3 us (68%)
  local copies, waits for them, and re-layouts  33.4 us (28%)
  other arithmetic  3.47 us (3%)
    pallas_call x1, Pallas kernels, shards(): pl.pallas_call(product, out_shape=[jax.ShapeDtypeStruct((share,) + paired...  36.5 us
    unnamed x3, local copies, waits for them, and re-layouts  29.6 us
    pallas_call x1, Pallas kernels, shards(): pl.pallas_call(exchange_first, out_shape=[jax.ShapeDtypeStruct((FACES, gh...  27.6 us
    pallas_call x1, Pallas kernels, shards(): pl.pallas_call(exchange_last, out_shape=jax.ShapeDtypeStruct((FACES, shar...  9.44 us
    pallas_call x1, Pallas kernels, shards(): pl.pallas_call(add_up, out_shape=jax.ShapeDtypeStruct((entries,) + paired...  3.87 us
    pallas_call x1, Pallas kernels, shards(): pl.pallas_call(pick_rows, out_shape=jax.ShapeDtypeStruct((layers * CAP,)...  2.83 us

profile of v2, /device:TPU:0, one launch (start us, length us, event | category | flops | bytes accessed | tf_op | source)
XLA Modules:
  0.0 117.3 jit_solution(1972196387875481336)
XLA Ops:
  0.0 0.1 stack.27
  0.1 0.7 slice_bitcast_fusion
  0.8 0.1 broadcast_in_dim.38
  0.8 0.1 broadcast_in_dim.39
  0.9 0.7 and_select_fusion
  1.6 0.1 convert_reduce_fusion
  1.7 0.7 compare_select_fusion.2
  2.4 0.6 select_reduce_fusion.index_ref
  3.0 0.8 slice_reduce_fusion.1
  3.8 0.1 slice.14
  3.9 0.7 reduce
  4.6 0.6 reshape.27.lists_ref
  5.2 0.6 pad.4.numbers_ref
  5.8 3.4 %copy.13 = bf16[32,8,32,128]{3,2,1,0:T(8,128)(2,1)} copy(bf16[32,8,32,128]{3,1,2,0:T(8,128)(2,1)} %bitcast.24) | data formatting | bytes 4194304
  9.3 23.3 %copy.11.blocks_ref = bf16[256,64,448]{2,1,0:T(8,128)(2,1)} copy(bf16[256,64,448]{0,2,1:T(8,128)(2,1)} %param.8) | data formatting | bytes 29360128 | tf_op args[0]
  32.6 2.8 %pick_rows.1.leaving_ref = bf16[12,64,448]{2,1,0:T(8,128)(2,1)} custom-call(s32[12]{0:T(128)} %select_reduce_fusion.index_ref, bf16[256,64,448]{2,1,0:T(8,128)(2,1)} %copy.11.blocks_ref), custom_call_target="tpu_custom_call" | custom-call | tf_op jit(solution)/shard_map/pick_rows/pallas_call | solution.py:334
  35.5 27.6 %exchange_first.1 = (bf16[6,64,32,128]{3,2,1,0:T(8,128)(2,1)}, bf16[12,64,448]{2,1,0:T(8,128)(2,1)}, s32[6,8,128]{2,1,0:T(8,128)}) custom-call(s32[384]{0:T(512)} %reshape.27.lists_ref, bf16[256,32,128]{2,1,0:T(8,128)(2,1)} %bitcast.19, bf16[12,64,448]{2,1,0:T(8,128)(2,1)} %pick_rows.1.leaving_ref, s32[6,8,128]{2,1,0:T(8,128)} %pad.4.numbers_ref), custom_call_target="tpu_custom_call" | custom-call | tf_op jit(solution)/shard_map/exchange_first/pallas_call | solution.py:346
  63.1 0.8 slice_reduce_fusion
  63.9 0.1 squeeze.7
  63.9 0.6 pad_add_fusion.entry_ref
  64.6 36.5 %product.1 = (f32[32,32,128]{2,1,0:T(8,128)}, bf16[192,32,128]{2,1,0:T(8,128)(2,1)}) custom-call(s32[256]{0:T(256)} %arrival_ref.1, s32[7,256]{1,0:T(8,128)} %bitcast.26, s32[7,256]{1,0:T(8,128)} %bitcast.27, bf16[256,32,128]{2,1,0:T(8,128)(2,1)} %bitcast.20, bf16[384,32,128]{2,1,0:T(8,128)(2,1)} %bitcast.23, bf16[256,64,448]{2,1,0:T(8,128)(2,1)} %copy.11.blocks_ref, ...), custom_call_target="tpu_custom_call" | custom-call | tf_op jit(solution)/shard_map/product/pallas_call | solution.py:365
  101.1 9.4 %exchange_last.1 = bf16[6,32,32,128]{3,2,1,0:T(8,128)(2,1)} custom-call(bf16[6,32,32,128]{3,2,1,0:T(8,128)(2,1)} %bitcast.25), custom_call_target="tpu_custom_call" | custom-call | tf_op jit(solution)/shard_map/exchange_last/pallas_call | solution.py:387
  110.6 3.9 %add_up.1 = f32[64,32,128]{2,1,0:T(8,128)} custom-call(s32[224]{0:T(256)} %pad_add_fusion.entry_ref, f32[32,32,128]{2,1,0:T(8,128)} %get-tuple-element.13.kept_ref, bf16[192,32,128]{2,1,0:T(8,128)(2,1)} %bitcast.21), custom_call_target="tpu_custom_call" | custom-call | tf_op jit(solution)/shard_map/add_up/pallas_call | solution.py:400
  114.5 2.8 %copy.16 = f32[8,8,32,128]{3,1,2,0:T(8,128)} copy(f32[8,8,32,128]{3,2,1,0:T(8,128)} %bitcast.22) | data formatting | bytes 2097152
  (1 shorter events, 0.0 us)
